TPU v7x, 32 devices: a whole 2x2x4 slice. The times are simulated.
32 devices in a mesh: rve: 8 (over z, core), slab: 4 (over y, x).
Axes of the slice: x: 2, y: 2, z: 4, core: 2. Of those that a mesh axis runs over, the one named last changes fastest.
Arguments:
- phase_ids: int32 [64, 4096], P('slab'), may hold values from 0 to 1, as said below
- yield_flags: int32 [8, 3, 64, 4096], P('rve', None, 'slab'), may hold values from 0 to 1
- plastic_strain: float32 [8, 6, 64, 4096], P('rve', None, 'slab'), may hold values from -0.03 to 0.03
- displacements: float32 [8, 3], replicated, may hold values from -0.06 to 0.06
- connectivity: int32 [1, 8], replicated, may hold values from 0 to 7, as said below
Outputs:
- gauss_stress: float32 [8, 6], P('rve')
- gauss_tangent: float32 [8, 6, 6], P('rve')
- nodal_forces: float32 [8, 3], replicated
- stiffness: float32 [24, 24], replicated
Inputs may be any that keep to these rules, and one draw needn't show every extreme that they name: `phase_ids`: 0 marks ferrite, 1 martensite. `connectivity`: element e is the cube [e, e+1] x [0,1] x [0,1]; entry c of its row is the id of its corner (e + c % 2, c // 2 % 2, c // 4); each point of the mesh has one id, distinct points distinct ids.
All inputs are finite; a program needn't handle non-finite values.
Results may differ from a plain program's by a relative error of at most 0.0001.
Values sent between devices are 32-bit elements; how exact they have to be, the bound alone decides.
A program may use at most 128 MiB of HBM per device.

v0:
```python
import math

import jax
import jax.numpy as jnp
import numpy as np
from jax import lax
from jax.experimental import pallas as pl
from jax.experimental.pallas import tpu as pltpu
from jax.sharding import PartitionSpec as P

GRID = 64
ITERS = 2


SHEAR_MODULUS = 80.0
BULK_MODULUS = 160.0
REFERENCE_SHEAR = 80.0
REFERENCE_LAME = 160.0 - 160.0 / 3.0
TANGENT_UNIT = 100.0
QUADRATURE_WEIGHT = 0.125
DIAGONAL_PART = (1.0, 1.0, 1.0, 0.0, 0.0, 0.0)
PAIR_WEIGHTS = (1.0, 1.0, 1.0, 2.0, 2.0, 2.0)
TENSOR_PAIRS = ((0, 0), (1, 1), (2, 2), (1, 2), (0, 2), (0, 1))
TENSOR_ROWS = ((0, 5, 4), (5, 1, 3), (4, 3, 2))


def gradient_table():
    inverse_root = 1.0 / math.sqrt(3.0)
    table_rows = np.zeros((8, 6, 24))
    for gauss_corner in range(8):
        position = [
            0.5 + (2 * (gauss_corner >> axis_number & 1) - 1) * 0.5 * inverse_root
            for axis_number in range(3)
        ]
        for corner in range(8):
            corner_bits = [corner >> axis_number & 1 for axis_number in range(3)]
            factors = [
                position[axis_number] * corner_bits[axis_number]
                + (1.0 - position[axis_number]) * (1 - corner_bits[axis_number])
                for axis_number in range(3)
            ]
            slopes = []
            for axis_number in range(3):
                slope_value = 2.0 * corner_bits[axis_number] - 1.0
                for other_axis in range(3):
                    if other_axis != axis_number:
                        slope_value = slope_value * factors[other_axis]
                slopes.append(slope_value)
            column = 3 * corner
            table_rows[gauss_corner, 0, column] += slopes[0]
            table_rows[gauss_corner, 1, column + 1] += slopes[1]
            table_rows[gauss_corner, 2, column + 2] += slopes[2]
            table_rows[gauss_corner, 3, column + 1] += 0.5 * slopes[2]
            table_rows[gauss_corner, 3, column + 2] += 0.5 * slopes[1]
            table_rows[gauss_corner, 4, column] += 0.5 * slopes[2]
            table_rows[gauss_corner, 4, column + 2] += 0.5 * slopes[0]
            table_rows[gauss_corner, 5, column] += 0.5 * slopes[1]
            table_rows[gauss_corner, 5, column + 1] += 0.5 * slopes[0]
    return table_rows


def point_geometry(points, connectivity, corner_lookup, node_count):
    element_count = connectivity.shape[0]
    point_count = points.shape[0]
    corner_selector = (points[:, None] % 8 == jnp.arange(8, dtype=jnp.int32)[None, :]).astype(
        jnp.float32
    )
    strain_row_values = jnp.einsum(
        "zu,utf->ztf", corner_selector, corner_lookup, precision=lax.Precision.HIGHEST
    )
    element_onehot = points[:, None] // 8 == jnp.arange(element_count, dtype=jnp.int32)[None, :]
    corner_nodes = jnp.sum(
        jnp.where(element_onehot[:, :, None], connectivity[None, :, :], 0), axis=1
    )
    degrees = 3 * corner_nodes[:, :, None] + jnp.arange(3, dtype=jnp.int32)[None, None, :]
    degrees = degrees.reshape(point_count, 24)
    placing = (
        degrees[:, :, None] == jnp.arange(3 * node_count, dtype=jnp.int32)[None, None, :]
    ).astype(jnp.float32)
    return (strain_row_values, placing)


def macro_strains(strain_row_values, placing, displacements):
    nodal_quantities = jnp.einsum(
        "gpn,n->gp", placing, displacements.reshape(-1), precision=lax.Precision.HIGHEST
    )
    return jnp.einsum(
        "vxw,vw->vx", strain_row_values, nodal_quantities, precision=lax.Precision.HIGHEST
    )


def material_response(strain, plastic, phase_ids, flag_values):
    diagonal = jnp.asarray(DIAGONAL_PART, jnp.float32)[:, None]
    weights = jnp.asarray(PAIR_WEIGHTS, jnp.float32)[:, None]
    martensite = phase_ids == 1
    yield_stress = jnp.where(martensite, 1.2, 0.3).astype(jnp.float32)
    hardening = jnp.where(martensite, 10.0, 2.0).astype(jnp.float32)
    elastic = strain - plastic
    volume = elastic[0] + elastic[1] + elastic[2]
    trial_dev = 2.0 * SHEAR_MODULUS * (elastic - diagonal * (volume / 3.0))
    equivalent = jnp.sqrt(1.5 * jnp.sum(weights * trial_dev * trial_dev, axis=0))
    bounded = jnp.maximum(equivalent, yield_stress)
    return_ratio = 3.0 * SHEAR_MODULUS / (3.0 * SHEAR_MODULUS + hardening)
    active = flag_values.astype(jnp.float32)
    plastic_flow = active * (equivalent - yield_stress) / bounded
    softening = 1.0 - return_ratio * plastic_flow
    stress = trial_dev * softening + diagonal * (BULK_MODULUS * volume)
    shear_term = 2.0 * SHEAR_MODULUS * softening
    tangent_weight = (
        3.0 * SHEAR_MODULUS * return_ratio * active * yield_stress / (bounded * bounded * bounded)
    )
    return (stress, trial_dev, shear_term, tangent_weight)


def wave_terms(index_x, index_y, index_z):
    middle = GRID // 2
    signed = []
    for indices in (index_x, index_y, index_z):
        wrapped = jnp.where(indices < middle, indices, indices - GRID)
        signed.append(jnp.where(indices == middle, 0, wrapped))
    nyquist_free = (index_x != middle) & (index_y != middle) & (index_z != middle)
    length = signed[0] * signed[0] + signed[1] * signed[1] + signed[2] * signed[2]
    keep_mask = (nyquist_free & (length > 0)).astype(jnp.float32)
    inverse_length = 1.0 / jnp.sqrt(jnp.maximum(length, 1).astype(jnp.float32))
    normals = [signed_entry.astype(jnp.float32) * inverse_length for signed_entry in signed]
    return (normals, keep_mask)


def project_green(components, normals, keep_mask):
    traction = [
        components[tensor_row[0]] * normals[0]
        + components[tensor_row[1]] * normals[1]
        + components[tensor_row[2]] * normals[2]
        for tensor_row in TENSOR_ROWS
    ]
    normal_load = normals[0] * traction[0] + normals[1] * traction[1] + normals[2] * traction[2]
    coupling = (REFERENCE_LAME + REFERENCE_SHEAR) / (
        REFERENCE_SHEAR * (REFERENCE_LAME + 2.0 * REFERENCE_SHEAR)
    )
    result_list = []
    for left_axis, right_axis in TENSOR_PAIRS:
        entry_value = (
            normals[left_axis] * traction[right_axis] + normals[right_axis] * traction[left_axis]
        ) / (2.0 * REFERENCE_SHEAR)
        entry_value = (
            entry_value - coupling * normals[left_axis] * normals[right_axis] * normal_load
        )
        result_list.append(entry_value * keep_mask)
    return jnp.stack(result_list)


def tangent_matrix(mean_shear, outer_sum):
    diagonal = jnp.asarray(DIAGONAL_PART, jnp.float32)
    volumetric = diagonal[:, None] * diagonal[None, :]
    weights = jnp.asarray(PAIR_WEIGHTS, jnp.float32)
    identity = jnp.eye(6, dtype=jnp.float32)
    whole = (
        BULK_MODULUS * volumetric
        + mean_shear * (identity - volumetric / 3.0)
        - outer_sum * weights[None, :]
    )
    return whole / TANGENT_UNIT


def assemble(stress_values, tangent_moduli, strain_row_values, placing):
    weights = jnp.asarray(PAIR_WEIGHTS, jnp.float32)
    force_row_values = strain_row_values * weights[None, :, None]
    element_force_vector = QUADRATURE_WEIGHT * jnp.einsum(
        "mbh,mb->mh", force_row_values, stress_values, precision=lax.Precision.HIGHEST
    )
    element_stiffness_matrix = QUADRATURE_WEIGHT * jnp.einsum(
        "xoh,xon,xnv->xhv",
        force_row_values,
        tangent_moduli,
        strain_row_values,
        precision=lax.Precision.HIGHEST,
    )
    forces = jnp.einsum("gp,gpn->n", element_force_vector, placing, precision=lax.Precision.HIGHEST)
    stiffness = jnp.einsum(
        "gpq,gpm,gqn->mn",
        element_stiffness_matrix,
        placing,
        placing,
        precision=lax.Precision.HIGHEST,
    )
    return (forces.reshape(-1, 3), stiffness)


def angle_table(count_rows, count_cols):
    rows_index = lax.broadcasted_iota(jnp.int32, (count_rows, count_cols), 0)
    cols_index = lax.broadcasted_iota(jnp.int32, (count_rows, count_cols), 1)
    angles = 2.0 * math.pi / GRID * (rows_index * cols_index % GRID).astype(jnp.float32)
    return (jnp.cos(angles), jnp.sin(angles))


def complex_table(inverse):
    cosine, sine = angle_table(GRID, GRID)
    if inverse:
        first_row = jnp.stack([cosine, -sine], axis=1)
        second_row = jnp.stack([sine, cosine], axis=1)
    else:
        first_row = jnp.stack([cosine, sine], axis=1)
        second_row = jnp.stack([-sine, cosine], axis=1)
    return jnp.stack([first_row, second_row], axis=0)


def on_device(phase_ids, yield_flags, plastic_strain, displacements, connectivity):
    slabs = lax.axis_size("slab")
    slab_index = lax.axis_index("slab")
    plane_count = phase_ids.shape[0]
    row_planes = GRID // slabs
    node_count = displacements.shape[0]
    corner_lookup = jnp.asarray(gradient_table(), jnp.float32)
    gauss_point = lax.axis_index("rve")
    own_points = jnp.full((1,), gauss_point, jnp.int32)
    strain_row_values, placing = point_geometry(own_points, connectivity, corner_lookup, node_count)
    macro_strain = macro_strains(strain_row_values, placing, displacements)[0]
    phases = phase_ids.reshape(-1)
    plastic = plastic_strain[0].reshape(6, -1)
    point_flags = yield_flags[0]
    columns = GRID // 2
    kept_index = lax.broadcasted_iota(jnp.int32, (columns, 1), 0)
    column_weight = jnp.where(kept_index == 0, 1.0, 2.0).astype(jnp.float32)
    depth_cos, depth_sin = angle_table(columns, GRID)
    forward_depth = jnp.stack([depth_cos, -depth_sin], axis=0)
    inverse_depth = jnp.stack(
        [column_weight * depth_cos, -column_weight * depth_sin], axis=0
    ) / float(GRID**3)
    forward_plane = complex_table(False)
    inverse_plane = complex_table(True)
    index_x = lax.broadcasted_iota(jnp.int32, (GRID, 1, 1), 0)
    index_y = slab_index * row_planes + lax.broadcasted_iota(jnp.int32, (1, row_planes, 1), 1)
    index_z = lax.broadcasted_iota(jnp.int32, (1, 1, columns), 2)
    normals, keep_mask = wave_terms(index_x, index_y, index_z)
    strain = jnp.broadcast_to(macro_strain[:, None], plastic.shape)
    for iteration in range(ITERS):
        stress = material_response(strain, plastic, phases, point_flags[iteration].reshape(-1))[0]
        voxel_block = stress.reshape(6, plane_count, GRID, GRID)
        spectral = jnp.einsum(
            "pkz,cxyz->pcxyk", forward_depth, voxel_block, precision=lax.Precision.HIGHEST
        )
        spectral = jnp.einsum(
            "pjqy,qcxyk->pcxjk", forward_plane, spectral, precision=lax.Precision.HIGHEST
        )
        spectral = lax.all_to_all(spectral, "slab", split_axis=3, concat_axis=2, tiled=True)
        spectral = jnp.einsum(
            "pjqx,qcxyk->pcjyk", forward_plane, spectral, precision=lax.Precision.HIGHEST
        )
        projected = project_green(
            [spectral[:, component] for component in range(6)], normals, keep_mask
        )
        spectral = jnp.einsum(
            "pjqx,cqxyk->pcjyk", inverse_plane, projected, precision=lax.Precision.HIGHEST
        )
        spectral = lax.all_to_all(spectral, "slab", split_axis=2, concat_axis=3, tiled=True)
        spectral = jnp.einsum(
            "pjqy,qcxyk->pcxjk", inverse_plane, spectral, precision=lax.Precision.HIGHEST
        )
        correction = jnp.einsum(
            "pkz,pcxyk->cxyz", inverse_depth, spectral, precision=lax.Precision.HIGHEST
        )
        strain = strain - correction.reshape(6, -1)
    stress, trial_dev, shear_term, tangent_weight = material_response(
        strain, plastic, phases, point_flags[ITERS].reshape(-1)
    )
    outer_part = jnp.dot(
        trial_dev * tangent_weight[None, :], trial_dev.T, precision=lax.Precision.HIGHEST
    )
    stress_total, shear_total, outer_total = lax.psum(
        (jnp.sum(stress, axis=1), jnp.sum(shear_term), outer_part), "slab"
    )
    voxel_count = float(GRID**3)
    mean_stress = stress_total / voxel_count
    tangent = tangent_matrix(shear_total / voxel_count, outer_total / voxel_count)
    own_forces, own_stiffness = assemble(
        mean_stress[None], tangent[None], strain_row_values, placing
    )
    forces, stiffness = lax.psum((own_forces, own_stiffness), "rve")
    return (mean_stress[None], tangent[None], forces, stiffness)


ROUGH = 16
GROUPS = 4
LANES = 128
STATS = 32
MESH = pl.DeviceIdType.MESH


def halves(value):
    high = value.astype(jnp.bfloat16)
    return high, (value - high.astype(jnp.float32)).astype(jnp.bfloat16)


def mul(left, right):
    return jnp.dot(left, right, preferred_element_type=jnp.float32)


def host_halves(table):
    table = np.asarray(table, np.float32)
    high = table.astype(jnp.bfloat16)
    low = (table - high.astype(np.float32)).astype(jnp.bfloat16)
    return jnp.asarray(np.stack([high, low]))


def depth_tables():
    kept = GRID // 2
    angles = 2.0 * np.pi / GRID * (np.arange(GRID)[:, None] * np.arange(kept)[None, :] % GRID)
    weight = np.where(np.arange(kept) == 0, 1.0, 2.0) / float(GRID**3)
    eye = np.eye(GROUPS)
    forward = np.concatenate([np.kron(eye, np.cos(angles)), np.kron(eye, -np.sin(angles))], axis=1)
    back_cos = (np.cos(angles) * weight[None, :]).T
    back_sin = (-np.sin(angles) * weight[None, :]).T
    inverse = np.concatenate([np.kron(eye, back_cos), np.kron(eye, back_sin)], axis=0)
    return forward, inverse


def line_tables():
    angles = 2.0 * np.pi / GRID * (np.arange(GRID)[:, None] * np.arange(GRID)[None, :] % GRID)
    cosine, sine = np.cos(angles), np.sin(angles)
    forward = np.block([[cosine, sine], [-sine, cosine]])
    inverse = np.block([[cosine, -sine], [sine, cosine]])
    return forward, inverse


def twiddle_table():
    lane_group = np.arange(LANES) // (LANES // GROUPS)
    angles = 2.0 * np.pi / GRID * (np.arange(ROUGH)[:, None] * lane_group[None, :])
    return jnp.asarray(np.stack([np.cos(angles), -np.sin(angles)], axis=1), jnp.float32)


def four_point(re, im, sign):
    a_re, a_im = re[0] + re[2], im[0] + im[2]
    b_re, b_im = re[0] - re[2], im[0] - im[2]
    c_re, c_im = re[1] + re[3], im[1] + im[3]
    d_re, d_im = re[1] - re[3], im[1] - im[3]
    e_re, e_im = (d_im, -d_re) if sign < 0 else (-d_im, d_re)
    return (
        [a_re + c_re, b_re + e_re, a_re - c_re, b_re - e_re],
        [a_im + c_im, b_im + e_im, a_im - c_im, b_im - e_im],
    )


def sixteen_point(re, im, sign):
    inner_re, inner_im = [], []
    for b in range(4):
        part_re, part_im = four_point(re[b::4], im[b::4], sign)
        for ka in range(1, 4):
            if b:
                angle = 2.0 * math.pi * b * ka / 16.0
                cosine, sine = math.cos(angle), sign * math.sin(angle)
                old_re, old_im = part_re[ka], part_im[ka]
                part_re[ka] = old_re * cosine - old_im * sine
                part_im[ka] = old_re * sine + old_im * cosine
        inner_re.append(part_re)
        inner_im.append(part_im)
    out_re, out_im = [None] * 16, [None] * 16
    for ka in range(4):
        part_re, part_im = four_point(
            [inner_re[b][ka] for b in range(4)], [inner_im[b][ka] for b in range(4)], sign
        )
        for kb in range(4):
            out_re[ka + 4 * kb] = part_re[kb]
            out_im[ka + 4 * kb] = part_im[kb]
    return out_re, out_im


def voxel_law(elastic, phase, flag, want_tangent):
    martensite = phase == 1
    yield_stress = jnp.where(martensite, 1.2, 0.3).astype(jnp.float32)
    base = 3.0 * SHEAR_MODULUS
    ratio = jnp.where(martensite, base / (base + 10.0), base / (base + 2.0)).astype(jnp.float32)
    volume = elastic[0] + elastic[1] + elastic[2]
    third = volume * (1.0 / 3.0)
    trial = [
        (2.0 * SHEAR_MODULUS) * (elastic[n] - third if n < 3 else elastic[n]) for n in range(6)
    ]
    square = [value * value for value in trial]
    norm = square[0] + square[1] + square[2] + 2.0 * (square[3] + square[4] + square[5])
    equivalent = jnp.sqrt(1.5 * norm)
    bounded = jnp.maximum(equivalent, yield_stress)
    active = flag.astype(jnp.float32)
    inverse = 1.0 / bounded
    active_ratio = active * ratio
    softening = 1.0 - active_ratio * ((equivalent - yield_stress) * inverse)
    pressure = BULK_MODULUS * volume
    stress = [trial[n] * softening + pressure if n < 3 else trial[n] * softening for n in range(6)]
    if not want_tangent:
        return stress
    beta = base * active_ratio * yield_stress * (inverse * inverse * inverse)
    return stress, trial, (2.0 * SHEAR_MODULUS) * softening, beta


def cell_kernel(
    slabs, points, macro_ref, phase_ref, flag_ref, plastic_ref, depth_ref, depth_back_ref,
    line_ref, line_back_ref, twiddle_ref, out_ref,
    elastic, planes, lines, lines_back, planes_back, work, sums, slab_sums, point_sums,
    send_sem, recv_sem, slab_send, slab_recv, point_send, point_recv,
):
    slab = lax.axis_index("slab")
    point = lax.axis_index("rve")
    rows = GRID // slabs
    own_lines = ROUGH // slabs
    wide = GROUPS * GRID

    barrier = pltpu.get_barrier_semaphore()
    for step in range(1, slabs):
        pl.semaphore_signal(
            barrier, inc=1, device_id={"slab": lax.rem(slab + step, slabs)}, device_id_type=MESH
        )
    for step in range(1, points):
        pl.semaphore_signal(
            barrier, inc=1, device_id={"rve": lax.rem(point + step, points)}, device_id_type=MESH
        )

    def lane_block(index):
        return pl.ds(pl.multiple_of(index * wide, wide), wide)

    def row_block(index):
        return pl.ds(pl.multiple_of(index * rows, rows), rows)

    @pl.loop(0, ROUGH)
    def _(block):
        for n in range(6):
            elastic[n, :, lane_block(block)] = macro_ref[n] - plastic_ref[n, :, lane_block(block)]

    lane = lax.broadcasted_iota(jnp.int32, (1, LANES), 1)
    group = lane >> 5
    high_sign = jnp.where((group >> 1) == 0, 1.0, -1.0).astype(jnp.float32)
    low_sign = jnp.where((group & 1) == 0, 1.0, -1.0).astype(jnp.float32)
    low_first = (group & 1) == 0
    corner = group == 3

    def across_high(value):
        return pltpu.roll(value, 64, 1) + high_sign * value

    def across_low(value):
        partner = jnp.where(low_first, pltpu.roll(value, 96, 1), pltpu.roll(value, 32, 1))
        return partner + low_sign * value

    def groups_forward(re, im, cosine, sine):
        re, im = re * cosine - im * sine, re * sine + im * cosine
        re, im = across_high(re), across_high(im)
        re, im = jnp.where(corner, im, re), jnp.where(corner, -re, im)
        return across_low(re), across_low(im)

    def groups_back(re, im, cosine, sine):
        re, im = across_low(re), across_low(im)
        re, im = jnp.where(corner, -im, re), jnp.where(corner, re, im)
        re, im = across_high(re), across_high(im)
        return re * cosine + im * sine, im * cosine - re * sine

    def sixteen(ref, sign):
        @pl.loop(0, 6)
        def _(n):
            for half in range(rows // 8):
                part = pl.ds(half * 8, 8)
                re = [ref[n, 0, k, part, :] for k in range(ROUGH)]
                im = [ref[n, 1, k, part, :] for k in range(ROUGH)]
                re, im = sixteen_point(re, im, sign)
                for k in range(ROUGH):
                    ref[n, 0, k, part, :] = re[k]
                    ref[n, 1, k, part, :] = im[k]

    def forward_copy(step, chunk, target, source):
        return pltpu.make_async_remote_copy(
            src_ref=planes.at[:, :, target * own_lines + chunk],
            dst_ref=lines.at[:, :, chunk, row_block(source), :],
            send_sem=send_sem.at[0, step - 1, chunk],
            recv_sem=recv_sem.at[0, step - 1, chunk],
            device_id={"slab": target},
            device_id_type=MESH,
        )

    def back_copy(step, chunk, target, source):
        return pltpu.make_async_remote_copy(
            src_ref=lines_back.at[:, :, chunk, row_block(target), :],
            dst_ref=planes_back.at[:, :, source * own_lines + chunk],
            send_sem=send_sem.at[1, step - 1, chunk],
            recv_sem=recv_sem.at[1, step - 1, chunk],
            device_id={"slab": target},
            device_id_type=MESH,
        )

    def to(step):
        return lax.rem(slab + step, slabs)

    def come_from(step):
        return lax.rem(slab + slabs - step, slabs)

    coupling = (REFERENCE_LAME + REFERENCE_SHEAR) / (
        REFERENCE_SHEAR * (REFERENCE_LAME + 2.0 * REFERENCE_SHEAR)
    )
    middle = GRID // 2

    def signed(index):
        wrapped = jnp.where(index < middle, index, index - GRID)
        return jnp.where(index == middle, 0, wrapped)

    def line_stage(chunk):
        stacked = jnp.concatenate(
            [lines[n, :, chunk].reshape(2 * GRID, LANES) for n in range(6)], axis=1
        )
        high, low = halves(stacked)
        work[...] = mul(line_ref[0], high) + mul(line_ref[0], low) + mul(line_ref[1], high)
        index_y = slab * own_lines + chunk + ROUGH * ((group >> 1) + 2 * (group & 1))
        index_z = lane & (LANES // GROUPS - 1)
        freq_y = signed(index_y)
        freq_z = index_z

        @pl.loop(0, GRID // 8)
        def _(block):
            index_x = block * 8 + lax.broadcasted_iota(jnp.int32, (8, 1), 0)
            freq_x = signed(index_x)
            length = freq_x * freq_x + (freq_y * freq_y + freq_z * freq_z)
            keep = (index_x != middle) & (index_y != middle) & (length > 0)
            inverse = jnp.where(keep, 1.0 / jnp.maximum(length, 1).astype(jnp.float32), 0.0)
            scale = inverse * (1.0 / REFERENCE_SHEAR)
            along = coupling * inverse * inverse
            xi = [freq.astype(jnp.float32) for freq in (freq_x, freq_y, freq_z)]
            for part in range(2):
                picked = pl.ds(pl.multiple_of(part * GRID + block * 8, 8), 8)
                tau = [work[picked, n * LANES : (n + 1) * LANES] for n in range(6)]
                load = [
                    tau[row[0]] * xi[0] + tau[row[1]] * xi[1] + tau[row[2]] * xi[2]
                    for row in TENSOR_ROWS
                ]
                normal = (xi[0] * load[0] + xi[1] * load[1] + xi[2] * load[2]) * along
                field = [0.5 * (load[d] * scale - xi[d] * normal) for d in range(3)]
                for n, (left, right) in enumerate(TENSOR_PAIRS):
                    value = xi[left] * field[right] + xi[right] * field[left]
                    work[picked, n * LANES : (n + 1) * LANES] = value

        high, low = halves(work[...])
        result = (
            mul(line_back_ref[0], high) + mul(line_back_ref[0], low) + mul(line_back_ref[1], high)
        )
        for n in range(6):
            lines_back[n, :, chunk] = result[:, n * LANES : (n + 1) * LANES].reshape(
                2, GRID, LANES
            )

    @pl.loop(0, ITERS)
    def _(iteration):
        @pl.loop(0, ROUGH)
        def _(block):
            at = lane_block(block)
            stress = voxel_law(
                [elastic[n, :, at] for n in range(6)],
                phase_ref[:, at],
                flag_ref[iteration, :, at],
                False,
            )
            high, low = halves(jnp.concatenate(stress, axis=0))
            result = mul(high, depth_ref[0]) + mul(low, depth_ref[0]) + mul(high, depth_ref[1])
            for n in range(6):
                piece = result[n * rows : (n + 1) * rows]
                planes[n, 0, block] = piece[:, :LANES]
                planes[n, 1, block] = piece[:, LANES:]

        sixteen(planes, -1)

        @pl.when(iteration == 0)
        def _():
            pl.semaphore_wait(barrier, slabs - 1 + points - 1)

        for chunk in range(own_lines):
            for step in list(range(1, slabs)) + [0]:
                target = to(step)
                line = target * own_lines + chunk
                cosine, sine = twiddle_ref[line, 0:1, :], twiddle_ref[line, 1:2, :]
                for n in range(6):
                    re, im = groups_forward(
                        planes[n, 0, line], planes[n, 1, line], cosine, sine
                    )
                    if step:
                        planes[n, 0, line] = re
                        planes[n, 1, line] = im
                    else:
                        lines[n, 0, chunk, row_block(slab), :] = re
                        lines[n, 1, chunk, row_block(slab), :] = im
                if step:
                    forward_copy(step, chunk, target, slab).start()

        @pl.loop(0, own_lines)
        def _(chunk):
            for step in range(1, slabs):
                forward_copy(step, chunk, to(step), come_from(step)).wait_recv()
            line_stage(chunk)
            for step in range(1, slabs):
                back_copy(step, chunk, to(step), slab).start()

        @pl.loop(0, own_lines)
        def _(chunk):
            for step in range(slabs):
                source = come_from(step)
                line = source * own_lines + chunk
                if step:
                    back_copy(step, chunk, to(step), source).wait_recv()
                cosine, sine = twiddle_ref[line, 0:1, :], twiddle_ref[line, 1:2, :]
                for n in range(6):
                    if step:
                        re, im = planes_back[n, 0, line], planes_back[n, 1, line]
                    else:
                        re = lines_back[n, 0, chunk, row_block(slab), :]
                        im = lines_back[n, 1, chunk, row_block(slab), :]
                    re, im = groups_back(re, im, cosine, sine)
                    planes_back[n, 0, line] = re
                    planes_back[n, 1, line] = im

        @pl.loop(0, own_lines)
        def _(chunk):
            for step in range(1, slabs):
                forward_copy(step, chunk, to(step), slab).wait_send()
                back_copy(step, chunk, to(step), slab).wait_send()

        sixteen(planes_back, 1)

        @pl.loop(0, ROUGH)
        def _(block):
            at = lane_block(block)
            stacked = jnp.concatenate(
                [
                    jnp.concatenate([planes_back[n, 0, block], planes_back[n, 1, block]], axis=1)
                    for n in range(6)
                ],
                axis=0,
            )
            high, low = halves(stacked)
            result = (
                mul(high, depth_back_ref[0])
                + mul(low, depth_back_ref[0])
                + mul(high, depth_back_ref[1])
            )
            for n in range(6):
                elastic[n, :, at] = elastic[n, :, at] - result[n * rows : (n + 1) * rows]

    sums[...] = jnp.zeros_like(sums)

    @pl.loop(0, ROUGH)
    def _(block):
        at = lane_block(block)
        stress, trial, shear, beta = voxel_law(
            [elastic[n, :, at] for n in range(6)], phase_ref[:, at], flag_ref[ITERS, :, at], True
        )
        entries = stress + [shear]
        for a in range(6):
            weighted = beta * trial[a]
            for b in range(a, 6):
                entries.append(weighted * trial[b])
        for place, value in enumerate(entries):
            folded = value[:, :LANES] + value[:, LANES:]
            total = folded[0:8]
            for half in range(1, rows // 8):
                total = total + folded[half * 8 : half * 8 + 8]
            sums[place] = sums[place] + total

    slab_sums[slab] = jnp.sum(sums[...], axis=1)

    def slab_copy(step, source):
        return pltpu.make_async_remote_copy(
            src_ref=slab_sums.at[source],
            dst_ref=slab_sums.at[source],
            send_sem=slab_send.at[step - 1],
            recv_sem=slab_recv.at[step - 1],
            device_id={"slab": to(step)},
            device_id_type=MESH,
        )

    def point_copy(step, source):
        return pltpu.make_async_remote_copy(
            src_ref=point_sums.at[source],
            dst_ref=point_sums.at[source],
            send_sem=point_send.at[step - 1],
            recv_sem=point_recv.at[step - 1],
            device_id={"rve": lax.rem(point + step, points)},
            device_id_type=MESH,
        )

    for step in range(1, slabs):
        slab_copy(step, slab).start()
    for step in range(1, slabs):
        slab_copy(step, come_from(step)).wait_recv()
    total = slab_sums[0]
    for other in range(1, slabs):
        total = total + slab_sums[other]
    point_sums[point] = jnp.broadcast_to(
        jnp.sum(total, axis=1, keepdims=True), (STATS, LANES)
    )
    for step in range(1, points):
        point_copy(step, point).start()
    for step in range(1, points):
        point_copy(step, lax.rem(point + points - step, points)).wait_recv()
    out_ref[...] = point_sums[...]
    for step in range(1, slabs):
        slab_copy(step, slab).wait_send()
    for step in range(1, points):
        point_copy(step, point).wait_send()


def fused_on_device(phase_ids, yield_flags, plastic_strain, displacements, connectivity):
    slabs = lax.axis_size("slab")
    points = lax.axis_size("rve")
    rows = phase_ids.shape[0]
    node_count = displacements.shape[0]
    element_count = connectivity.shape[0]
    own_lines = ROUGH // slabs
    point = lax.axis_index("rve")
    lookup = gradient_table()
    placing = (
        connectivity[:, :, None] == jnp.arange(node_count, dtype=jnp.int32)[None, None, :]
    ).astype(jnp.float32)
    corner_moves = jnp.sum(placing[:, :, :, None] * displacements[None, None, :, :], axis=2)
    all_strain = jnp.sum(
        jnp.asarray(lookup, jnp.float32)[None] * corner_moves.reshape(element_count, 1, 1, 24),
        axis=3,
    ).reshape(points, 6)
    macro_strain = lax.dynamic_slice(all_strain, (point, 0), (1, 6))[0]

    depth, depth_back = depth_tables()
    line, line_back = line_tables()
    wide = GROUPS * GRID
    vmem = pl.BlockSpec(memory_space=pltpu.VMEM)
    stats = pl.pallas_call(
        lambda *refs: cell_kernel(slabs, points, *refs),
        out_shape=jax.ShapeDtypeStruct((points, STATS, LANES), jnp.float32),
        in_specs=[pl.BlockSpec(memory_space=pltpu.SMEM)] + [vmem] * 8,
        out_specs=vmem,
        scratch_shapes=[
            pltpu.VMEM((6, rows, GRID * GRID), jnp.float32),
            pltpu.VMEM((6, 2, ROUGH, rows, LANES), jnp.float32),
            pltpu.VMEM((6, 2, own_lines, GRID, LANES), jnp.float32),
            pltpu.VMEM((6, 2, own_lines, GRID, LANES), jnp.float32),
            pltpu.VMEM((6, 2, ROUGH, rows, LANES), jnp.float32),
            pltpu.VMEM((2 * GRID, 6 * LANES), jnp.float32),
            pltpu.VMEM((STATS, 8, LANES), jnp.float32),
            pltpu.VMEM((slabs, STATS, LANES), jnp.float32),
            pltpu.VMEM((points, STATS, LANES), jnp.float32),
            pltpu.SemaphoreType.DMA((2, slabs - 1, own_lines)),
            pltpu.SemaphoreType.DMA((2, slabs - 1, own_lines)),
            pltpu.SemaphoreType.DMA((slabs - 1,)),
            pltpu.SemaphoreType.DMA((slabs - 1,)),
            pltpu.SemaphoreType.DMA((points - 1,)),
            pltpu.SemaphoreType.DMA((points - 1,)),
        ],
        compiler_params=pltpu.CompilerParams(
            collective_id=0, has_side_effects=True, vmem_limit_bytes=40 * 1024 * 1024
        ),
    )(
        macro_strain,
        phase_ids,
        yield_flags[0],
        plastic_strain[0],
        host_halves(depth),
        host_halves(depth_back),
        host_halves(line),
        host_halves(line_back),
        twiddle_table(),
    )
    means = stats[:, :, 0] / float(GRID**3)
    mean_stress = means[:, :6]
    pair_place = np.zeros((6, 6), np.int32)
    place = 7
    for a in range(6):
        for b in range(a, 6):
            pair_place[a, b] = pair_place[b, a] = place
            place += 1
    outer = jnp.stack([means[:, place] for place in pair_place.reshape(-1)], axis=1)
    outer = outer.reshape(points, 6, 6)
    tangent = jax.vmap(tangent_matrix)(means[:, 6], outer)
    weights = np.asarray(PAIR_WEIGHTS)
    weighted = lookup * weights[None, :, None] * QUADRATURE_WEIGHT
    weighted = jnp.asarray(weighted.reshape(48, 24), jnp.float32)
    element_force = jnp.sum(
        mean_stress.reshape(element_count, 48, 1) * weighted[None], axis=1
    )
    best = lax.Precision.HIGHEST
    spread = jnp.einsum(
        "equn,qnv->equv",
        tangent.reshape(element_count, 8, 6, 6),
        jnp.asarray(lookup, jnp.float32),
        precision=best,
    ).reshape(element_count, 48, 24)
    element_stiffness = jnp.einsum("rh,erv->ehv", weighted, spread, precision=best)
    forces = jnp.einsum(
        "eck,ecn->nk", element_force.reshape(element_count, 8, 3), placing, precision=best
    )
    block = element_stiffness.reshape(element_count, 8, 3, 8, 3)
    stiffness = jnp.einsum("ecn,eckdl,edm->nkml", placing, block, placing, precision=best)
    stiffness = stiffness.reshape(3 * node_count, 3 * node_count)
    own_stress = lax.dynamic_slice(mean_stress, (point, 0), (1, 6))
    own_tangent = lax.dynamic_slice(tangent, (point, 0, 0), (1, 6, 6))
    return (own_stress, own_tangent, forces, stiffness)


def solution(mesh):
    slabs = mesh.shape["slab"]
    fits = slabs > 1 and ROUGH % slabs == 0 and GRID // slabs % 8 == 0
    body = fused_on_device if fits else on_device
    return jax.shard_map(
        body,
        mesh=mesh,
        in_specs=(
            P("slab", None),
            P("rve", None, "slab", None),
            P("rve", None, "slab", None),
            P(),
            P(),
        ),
        out_specs=(P("rve", None), P("rve", None, None), P(), P()),
        check_vma=False,
    )
```

profile of v0, /device:TPU:0, one launch (start us, length us, event | category | flops | bytes accessed | tf_op | source)
XLA Modules:
  0.0 119.1 jit_solution(2146350723452997866)
XLA Ops:
  0.6 0.7 fusion.4
  1.4 0.8 multiply_reduce_fusion.3
  2.3 0.8 multiply_reduce_fusion.1
  3.2 1.4 %copy-done = f32[1,6,16,4096]{3,2,1,0:T(8,128)S(1)} copy-done((f32[1,6,16,4096]{3,2,1,0:T(8,128)S(1)}, f32[1,6,16,4096]{3,2,1,0:T(8,128)}, u32[]{:S(2)}) %copy-start) | copy-done | bytes 1572888
  4.6 1.1 copy-done.1
  5.7 0.9 copy-done.2
  6.6 0.9 copy-done.3
  7.6 0.9 copy-done.4
  8.5 0.8 copy-done.5
  9.4 0.8 copy-done.6
  10.2 0.7 copy-done.7
  11.0 102.6 %shard_map.174 = f32[8,32,128]{2,1,0:T(8,128)S(1)} custom-call(f32[6]{0:T(128)S(1)} %fusion.13.refs_0_, s32[16,4096]{1,0:T(8,128)S(1)} %copy-done.2, s32[3,16,4096]{2,1,0:T(8,128)S(1)} %bitcast.41, f32[6,16,4096]{2,1,0:T(8,128)S(1)} %bitcast.40, bf16[2,256,256]{2,1,0:T(8,128)(2,1)S(1)} %copy-done.3, bf16[2,256,256]{2,1,0:T(8,128)(2,1)S(1)} %copy-done.4, ...), custom_call_target="tpu_custom_call" | custom-call | tf_op jit(solution)/shard_map/pallas_call | solution.py:723
  113.7 0.5 constant_dynamic-slice_fusion.1
  114.3 0.2 slice_reduce_fusion
  115.1 0.6 copy.31
  115.8 0.1 multiply_reduce_fusion.2
  115.9 0.8 fusion.6
  116.8 0.2 convolution_bitcast_fusion.1
  117.0 0.2 convolution_bitcast_fusion.2
  117.3 0.2 copy.28
  117.5 0.4 fusion.8
  117.9 0.2 convolution_bitcast_fusion
  118.2 0.2 copy.30
  118.4 0.7 reshape.247
  (36 shorter events, 1.3 us)
Async XLA Ops:
  3.1 1.4 %copy-start = (f32[1,6,16,4096]{3,2,1,0:T(8,128)S(1)}, f32[1,6,16,4096]{3,2,1,0:T(8,128)}, u32[]{:S(2)}) copy-start(f32[1,6,16,4096]{3,2,1,0:T(8,128)} %param.17) | copy-start | bytes 4718596
  4.6 1.1 copy-start.1
  5.7 0.9 copy-start.2
  6.6 0.9 copy-start.3
  7.6 0.9 copy-start.4
  8.5 0.8 copy-start.5
  9.4 0.8 copy-start.6
  10.2 0.7 copy-start.7
  10.9 104.0 %copy-start.11 = (f32[6]{0:T(128)S(1)}, f32[6]{0:T(128)}, u32[]{:S(2)}) copy-start(f32[6]{0:T(128)} %constant.48.clone) | copy-start | bytes 76
  10.9 104.0 %copy-start.12 = (f32[6]{0:T(128)S(1)}, f32[6]{0:T(128)}, u32[]{:S(2)}) copy-start(f32[6]{0:T(128)} %constant.49.clone) | copy-start | bytes 76
  10.9 104.8 %copy-start.9 = (f32[48,24]{0,1:T(8,128)S(1)}, f32[48,24]{0,1:T(8,128)}, u32[]{:S(2)}) copy-start(f32[48,24]{0,1:T(8,128)} %constant.50.clone) | copy-start | bytes 13828
  10.9 105.0 %copy-start.10 = (s32[1,8]{1,0:T(1,128)S(1)}, s32[1,8]{1,0:T(1,128)}, u32[]{:S(2)}) copy-start(s32[1,8]{1,0:T(1,128)} %param.19) | copy-start | bytes 100
  11.0 105.8 %copy-start.8 = (f32[8,6,24]{2,1,0:T(8,128)S(1)}, f32[8,6,24]{2,1,0:T(8,128)}, u32[]{:S(2)}) copy-start(f32[8,6,24]{2,1,0:T(8,128)} %constant.42.clone) | copy-start | bytes 13828
where the time goes:
time: 120 us; the launch traced here: 119 us
  Pallas kernels  103 us (86%)
  local copies, waits for them, and re-layouts  11.2 us (9%)
  other arithmetic  2.71 us (2%)
  matrix products  1.87 us (2%)
    pallas_call x1, Pallas kernels, fused_on_device(): pl.pallas_call(lambda *refs: cell_kernel(slabs, points, *refs), out_shape...  103 us
    unnamed x27, local copies, waits for them, and re-layouts  8.38 us

commit v1 on v0

--- a/solution.py
+++ b/solution.py
@@ -299,7 +299,7 @@
     table = np.asarray(table, np.float32)
     high = table.astype(jnp.bfloat16)
     low = (table - high.astype(np.float32)).astype(jnp.bfloat16)
-    return jnp.asarray(np.stack([high, low]))
+    return np.stack([high, low])
 
 
 def depth_tables():
@@ -391,10 +391,11 @@
 
 
 def cell_kernel(
-    slabs, points, macro_ref, phase_ref, flag_ref, plastic_ref, depth_ref, depth_back_ref,
-    line_ref, line_back_ref, twiddle_ref, out_ref,
+    slabs, points, macro_ref, phase_hbm, flag_hbm, plastic_hbm, depth_hbm, line_hbm, twiddle_hbm,
+    out_ref,
+    phase_ref, flag_ref, depth_ref, line_ref, twiddle_ref,
     elastic, planes, lines, lines_back, planes_back, work, sums, slab_sums, point_sums,
-    send_sem, recv_sem, slab_send, slab_recv, point_send, point_recv,
+    load_sem, send_sem, recv_sem, slab_send, slab_recv, point_send, point_recv,
 ):
     slab = lax.axis_index("slab")
     point = lax.axis_index("rve")
@@ -418,10 +419,27 @@
     def row_block(index):
         return pl.ds(pl.multiple_of(index * rows, rows), rows)
 
-    @pl.loop(0, ROUGH)
-    def _(block):
-        for n in range(6):
-            elastic[n, :, lane_block(block)] = macro_ref[n] - plastic_ref[n, :, lane_block(block)]
+    parts = rows // 8
+
+    def part_rows(part):
+        return pl.ds(pl.multiple_of(part * 8, 8), 8)
+
+    pairs = [
+        (plastic_hbm.at[:, 0:8], elastic.at[:, 0:8]),
+        (phase_hbm, phase_ref),
+        (flag_hbm.at[0], flag_ref.at[0]),
+        (depth_hbm, depth_ref),
+        (twiddle_hbm, twiddle_ref),
+        (plastic_hbm.at[:, 8:rows], elastic.at[:, 8:rows]),
+        (line_hbm, line_ref),
+        (flag_hbm.at[1:], flag_ref.at[1:]),
+    ]
+    loads = [
+        pltpu.make_async_copy(source, target, load_sem.at[place])
+        for place, (source, target) in enumerate(pairs)
+    ]
+    for load in loads:
+        load.start()
 
     lane = lax.broadcasted_iota(jnp.int32, (1, LANES), 1)
     group = lane >> 5
@@ -449,34 +467,36 @@
         re, im = across_high(re), across_high(im)
         return re * cosine + im * sine, im * cosine - re * sine
 
-    def sixteen(ref, sign):
+    def sixteen(ref, sign, part):
         @pl.loop(0, 6)
         def _(n):
-            for half in range(rows // 8):
-                part = pl.ds(half * 8, 8)
-                re = [ref[n, 0, k, part, :] for k in range(ROUGH)]
-                im = [ref[n, 1, k, part, :] for k in range(ROUGH)]
-                re, im = sixteen_point(re, im, sign)
-                for k in range(ROUGH):
-                    ref[n, 0, k, part, :] = re[k]
-                    ref[n, 1, k, part, :] = im[k]
-
-    def forward_copy(step, chunk, target, source):
+            picked = part_rows(part)
+            re = [ref[n, 0, k, picked, :] for k in range(ROUGH)]
+            im = [ref[n, 1, k, picked, :] for k in range(ROUGH)]
+            re, im = sixteen_point(re, im, sign)
+            for k in range(ROUGH):
+                ref[n, 0, k, picked, :] = re[k]
+                ref[n, 1, k, picked, :] = im[k]
+
+    def slab_rows(index, part):
+        return pl.ds(pl.multiple_of(index * rows + part * 8, 8), 8)
+
+    def forward_copy(step, chunk, part, target, source):
         return pltpu.make_async_remote_copy(
-            src_ref=planes.at[:, :, target * own_lines + chunk],
-            dst_ref=lines.at[:, :, chunk, row_block(source), :],
-            send_sem=send_sem.at[0, step - 1, chunk],
-            recv_sem=recv_sem.at[0, step - 1, chunk],
+            src_ref=planes.at[:, :, target * own_lines + chunk, part_rows(part), :],
+            dst_ref=lines.at[:, :, chunk, slab_rows(source, part), :],
+            send_sem=send_sem.at[0, part, step - 1, chunk],
+            recv_sem=recv_sem.at[0, part, step - 1, chunk],
             device_id={"slab": target},
             device_id_type=MESH,
         )
 
-    def back_copy(step, chunk, target, source):
+    def back_copy(step, chunk, part, target, source):
         return pltpu.make_async_remote_copy(
-            src_ref=lines_back.at[:, :, chunk, row_block(target), :],
-            dst_ref=planes_back.at[:, :, source * own_lines + chunk],
-            send_sem=send_sem.at[1, step - 1, chunk],
-            recv_sem=recv_sem.at[1, step - 1, chunk],
+            src_ref=lines_back.at[:, :, chunk, slab_rows(target, part), :],
+            dst_ref=planes_back.at[:, :, source * own_lines + chunk, part_rows(part), :],
+            send_sem=send_sem.at[1, part, step - 1, chunk],
+            recv_sem=recv_sem.at[1, part, step - 1, chunk],
             device_id={"slab": target},
             device_id_type=MESH,
         )
@@ -501,7 +521,7 @@
             [lines[n, :, chunk].reshape(2 * GRID, LANES) for n in range(6)], axis=1
         )
         high, low = halves(stacked)
-        work[...] = mul(line_ref[0], high) + mul(line_ref[0], low) + mul(line_ref[1], high)
+        work[...] = mul(line_ref[0, 0], high) + mul(line_ref[0, 0], low) + mul(line_ref[0, 1], high)
         index_y = slab * own_lines + chunk + ROUGH * ((group >> 1) + 2 * (group & 1))
         index_z = lane & (LANES // GROUPS - 1)
         freq_y = signed(index_y)
@@ -532,62 +552,63 @@
 
         high, low = halves(work[...])
         result = (
-            mul(line_back_ref[0], high) + mul(line_back_ref[0], low) + mul(line_back_ref[1], high)
+            mul(line_ref[1, 0], high) + mul(line_ref[1, 0], low) + mul(line_ref[1, 1], high)
         )
         for n in range(6):
             lines_back[n, :, chunk] = result[:, n * LANES : (n + 1) * LANES].reshape(
                 2, GRID, LANES
             )
 
-    @pl.loop(0, ITERS)
-    def _(iteration):
-        @pl.loop(0, ROUGH)
-        def _(block):
-            at = lane_block(block)
-            stress = voxel_law(
-                [elastic[n, :, at] for n in range(6)],
-                phase_ref[:, at],
-                flag_ref[iteration, :, at],
-                False,
+    def twiddles(line):
+        return twiddle_ref[pl.ds(2 * line, 1), :], twiddle_ref[pl.ds(2 * line + 1, 1), :]
+
+    def plane_forward(iteration, part):
+        picked = part_rows(part)
+
+        @pl.loop(0, ROUGH // 4)
+        def _(batch):
+            pieces = []
+            for inner in range(4):
+                at = lane_block(batch * 4 + inner)
+                pieces += voxel_law(
+                    [elastic[n, picked, at] for n in range(6)],
+                    phase_ref[picked, at],
+                    flag_ref[iteration, picked, at],
+                    False,
+                )
+            high, low = halves(jnp.concatenate(pieces, axis=0))
+            result = (
+                mul(high, depth_ref[0, 0]) + mul(low, depth_ref[0, 0]) + mul(high, depth_ref[0, 1])
             )
-            high, low = halves(jnp.concatenate(stress, axis=0))
-            result = mul(high, depth_ref[0]) + mul(low, depth_ref[0]) + mul(high, depth_ref[1])
-            for n in range(6):
-                piece = result[n * rows : (n + 1) * rows]
-                planes[n, 0, block] = piece[:, :LANES]
-                planes[n, 1, block] = piece[:, LANES:]
-
-        sixteen(planes, -1)
-
-        @pl.when(iteration == 0)
-        def _():
-            pl.semaphore_wait(barrier, slabs - 1 + points - 1)
-
-        for chunk in range(own_lines):
+            for inner in range(4):
+                for n in range(6):
+                    first = (inner * 6 + n) * 8
+                    planes[n, 0, batch * 4 + inner, picked, :] = result[first : first + 8, :LANES]
+                    planes[n, 1, batch * 4 + inner, picked, :] = result[first : first + 8, LANES:]
+
+        sixteen(planes, -1, part)
+
+        @pl.loop(0, own_lines)
+        def _(chunk):
             for step in list(range(1, slabs)) + [0]:
                 target = to(step)
                 line = target * own_lines + chunk
-                cosine, sine = twiddle_ref[line, 0:1, :], twiddle_ref[line, 1:2, :]
+                cosine, sine = twiddles(line)
                 for n in range(6):
                     re, im = groups_forward(
-                        planes[n, 0, line], planes[n, 1, line], cosine, sine
+                        planes[n, 0, line, picked, :], planes[n, 1, line, picked, :], cosine, sine
                     )
                     if step:
-                        planes[n, 0, line] = re
-                        planes[n, 1, line] = im
+                        planes[n, 0, line, picked, :] = re
+                        planes[n, 1, line, picked, :] = im
                     else:
-                        lines[n, 0, chunk, row_block(slab), :] = re
-                        lines[n, 1, chunk, row_block(slab), :] = im
+                        lines[n, 0, chunk, slab_rows(slab, part), :] = re
+                        lines[n, 1, chunk, slab_rows(slab, part), :] = im
                 if step:
-                    forward_copy(step, chunk, target, slab).start()
-
-        @pl.loop(0, own_lines)
-        def _(chunk):
-            for step in range(1, slabs):
-                forward_copy(step, chunk, to(step), come_from(step)).wait_recv()
-            line_stage(chunk)
-            for step in range(1, slabs):
-                back_copy(step, chunk, to(step), slab).start()
+                    forward_copy(step, chunk, part, target, slab).start()
+
+    def plane_back(part):
+        picked = part_rows(part)
 
         @pl.loop(0, own_lines)
         def _(chunk):
@@ -595,64 +616,128 @@
                 source = come_from(step)
                 line = source * own_lines + chunk
                 if step:
-                    back_copy(step, chunk, to(step), source).wait_recv()
-                cosine, sine = twiddle_ref[line, 0:1, :], twiddle_ref[line, 1:2, :]
+                    back_copy(step, chunk, part, to(step), source).wait_recv()
+                cosine, sine = twiddles(line)
                 for n in range(6):
                     if step:
-                        re, im = planes_back[n, 0, line], planes_back[n, 1, line]
+                        re = planes_back[n, 0, line, picked, :]
+                        im = planes_back[n, 1, line, picked, :]
                     else:
-                        re = lines_back[n, 0, chunk, row_block(slab), :]
-                        im = lines_back[n, 1, chunk, row_block(slab), :]
+                        re = lines_back[n, 0, chunk, slab_rows(slab, part), :]
+                        im = lines_back[n, 1, chunk, slab_rows(slab, part), :]
                     re, im = groups_back(re, im, cosine, sine)
-                    planes_back[n, 0, line] = re
-                    planes_back[n, 1, line] = im
-
+                    planes_back[n, 0, line, picked, :] = re
+                    planes_back[n, 1, line, picked, :] = im
+
+        sixteen(planes_back, 1, part)
+
+        @pl.loop(0, ROUGH // 4)
+        def _(batch):
+            stacked = jnp.concatenate(
+                [
+                    jnp.concatenate(
+                        [
+                            planes_back[n, side, batch * 4 + inner, picked, :]
+                            for inner in range(4)
+                            for n in range(6)
+                        ],
+                        axis=0,
+                    )
+                    for side in range(2)
+                ],
+                axis=1,
+            )
+            high, low = halves(stacked)
+            result = (
+                mul(high, depth_ref[1, 0]) + mul(low, depth_ref[1, 0]) + mul(high, depth_ref[1, 1])
+            )
+            for inner in range(4):
+                at = lane_block(batch * 4 + inner)
+                for n in range(6):
+                    first = (inner * 6 + n) * 8
+                    elastic[n, picked, at] = elastic[n, picked, at] - result[first : first + 8]
+
+    def final_sums(part):
+        picked = part_rows(part)
+
+        @pl.loop(0, ROUGH)
+        def _(block):
+            at = lane_block(block)
+            stress, trial, shear, beta = voxel_law(
+                [elastic[n, picked, at] for n in range(6)],
+                phase_ref[picked, at],
+                flag_ref[ITERS, picked, at],
+                True,
+            )
+            entries = stress + [shear]
+            for a in range(6):
+                weighted = beta * trial[a]
+                for b in range(a, 6):
+                    entries.append(weighted * trial[b])
+            for place, value in enumerate(entries):
+                sums[place] = sums[place] + (value[:, :LANES] + value[:, LANES:])
+
+    sums[...] = jnp.zeros_like(sums)
+    for load in loads[:5]:
+        load.wait()
+
+    @pl.loop(0, parts)
+    def _(part):
+        @pl.when(part == 1)
+        def _():
+            loads[5].wait()
+
+        picked = part_rows(part)
+
+        @pl.loop(0, ROUGH)
+        def _(block):
+            at = lane_block(block)
+            for n in range(6):
+                elastic[n, picked, at] = macro_ref[n] - elastic[n, picked, at]
+
+        @pl.when(part == 0)
+        def _():
+            pl.semaphore_wait(barrier, slabs - 1 + points - 1)
+
+        plane_forward(0, part)
+
+    for load in loads[6:]:
+        load.wait()
+
+    @pl.loop(0, ITERS)
+    def _(iteration):
         @pl.loop(0, own_lines)
         def _(chunk):
             for step in range(1, slabs):
-                forward_copy(step, chunk, to(step), slab).wait_send()
-                back_copy(step, chunk, to(step), slab).wait_send()
-
-        sixteen(planes_back, 1)
-
-        @pl.loop(0, ROUGH)
-        def _(block):
-            at = lane_block(block)
-            stacked = jnp.concatenate(
-                [
-                    jnp.concatenate([planes_back[n, 0, block], planes_back[n, 1, block]], axis=1)
-                    for n in range(6)
-                ],
-                axis=0,
-            )
-            high, low = halves(stacked)
-            result = (
-                mul(high, depth_back_ref[0])
-                + mul(low, depth_back_ref[0])
-                + mul(high, depth_back_ref[1])
-            )
-            for n in range(6):
-                elastic[n, :, at] = elastic[n, :, at] - result[n * rows : (n + 1) * rows]
-
-    sums[...] = jnp.zeros_like(sums)
-
-    @pl.loop(0, ROUGH)
-    def _(block):
-        at = lane_block(block)
-        stress, trial, shear, beta = voxel_law(
-            [elastic[n, :, at] for n in range(6)], phase_ref[:, at], flag_ref[ITERS, :, at], True
-        )
-        entries = stress + [shear]
-        for a in range(6):
-            weighted = beta * trial[a]
-            for b in range(a, 6):
-                entries.append(weighted * trial[b])
-        for place, value in enumerate(entries):
-            folded = value[:, :LANES] + value[:, LANES:]
-            total = folded[0:8]
-            for half in range(1, rows // 8):
-                total = total + folded[half * 8 : half * 8 + 8]
-            sums[place] = sums[place] + total
+                for part in range(parts):
+                    forward_copy(step, chunk, part, to(step), come_from(step)).wait_recv()
+            line_stage(chunk)
+            for step in range(1, slabs):
+                back_copy(step, chunk, 0, to(step), slab).start()
+
+        @pl.loop(0, own_lines)
+        def _(chunk):
+            for part in range(1, parts):
+                for step in range(1, slabs):
+                    back_copy(step, chunk, part, to(step), slab).start()
+
+        @pl.loop(0, parts)
+        def _(part):
+            plane_back(part)
+
+            @pl.loop(0, own_lines)
+            def _(chunk):
+                for step in range(1, slabs):
+                    forward_copy(step, chunk, part, to(step), slab).wait_send()
+                    back_copy(step, chunk, part, to(step), slab).wait_send()
+
+            @pl.when(iteration < ITERS - 1)
+            def _():
+                plane_forward(iteration + 1, part)
+
+            @pl.when(iteration == ITERS - 1)
+            def _():
+                final_sums(part)
 
     slab_sums[slab] = jnp.sum(sums[...], axis=1)
 
@@ -723,9 +808,15 @@
     stats = pl.pallas_call(
         lambda *refs: cell_kernel(slabs, points, *refs),
         out_shape=jax.ShapeDtypeStruct((points, STATS, LANES), jnp.float32),
-        in_specs=[pl.BlockSpec(memory_space=pltpu.SMEM)] + [vmem] * 8,
+        in_specs=[pl.BlockSpec(memory_space=pltpu.SMEM)]
+        + [pl.BlockSpec(memory_space=pltpu.HBM)] * 6,
         out_specs=vmem,
         scratch_shapes=[
+            pltpu.VMEM((rows, GRID * GRID), jnp.int32),
+            pltpu.VMEM((ITERS + 1, rows, GRID * GRID), jnp.int32),
+            pltpu.VMEM((2, 2, wide, wide), jnp.bfloat16),
+            pltpu.VMEM((2, 2, 2 * GRID, 2 * GRID), jnp.bfloat16),
+            pltpu.VMEM((2 * ROUGH, LANES), jnp.float32),
             pltpu.VMEM((6, rows, GRID * GRID), jnp.float32),
             pltpu.VMEM((6, 2, ROUGH, rows, LANES), jnp.float32),
             pltpu.VMEM((6, 2, own_lines, GRID, LANES), jnp.float32),
@@ -735,8 +826,9 @@
             pltpu.VMEM((STATS, 8, LANES), jnp.float32),
             pltpu.VMEM((slabs, STATS, LANES), jnp.float32),
             pltpu.VMEM((points, STATS, LANES), jnp.float32),
-            pltpu.SemaphoreType.DMA((2, slabs - 1, own_lines)),
-            pltpu.SemaphoreType.DMA((2, slabs - 1, own_lines)),
+            pltpu.SemaphoreType.DMA((8,)),
+            pltpu.SemaphoreType.DMA((2, rows // 8, slabs - 1, own_lines)),
+            pltpu.SemaphoreType.DMA((2, rows // 8, slabs - 1, own_lines)),
             pltpu.SemaphoreType.DMA((slabs - 1,)),
             pltpu.SemaphoreType.DMA((slabs - 1,)),
             pltpu.SemaphoreType.DMA((points - 1,)),
@@ -750,11 +842,9 @@
         phase_ids,
         yield_flags[0],
         plastic_strain[0],
-        host_halves(depth),
-        host_halves(depth_back),
-        host_halves(line),
-        host_halves(line_back),
-        twiddle_table(),
+        jnp.asarray(np.stack([host_halves(depth), host_halves(depth_back)])),
+        jnp.asarray(np.stack([host_halves(line), host_halves(line_back)])),
+        twiddle_table().reshape(2 * ROUGH, LANES),
     )
     means = stats[:, :, 0] / float(GRID**3)
     mean_stress = means[:, :6]
@@ -794,7 +884,7 @@
 
 def solution(mesh):
     slabs = mesh.shape["slab"]
-    fits = slabs > 1 and ROUGH % slabs == 0 and GRID // slabs % 8 == 0
+    fits = slabs > 1 and ROUGH % slabs == 0 and GRID // slabs % 16 == 0
     body = fused_on_device if fits else on_device
     return jax.shard_map(
         body,

time: 120 us -> 103 us (0.86)
  Pallas kernels: 103 us -> 87.3 us
  local copies, waits for them, and re-layouts: 11.2 us -> 9.54 us
    pallas_call x1, Pallas kernels: 103 us -> 87.3 us  [fused_on_device(): pl.pallas_call(lambda *refs: cell_kernel(slabs, points, *refs), out_shape...]
    unnamed x27 -> x23, local copies, waits for them, and re-layouts: 8.38 us -> 6.75 us
where the time goes in v1:
time: 103 us; the launch traced here: 102 us
  Pallas kernels  87.3 us (85%)
  local copies, waits for them, and re-layouts  9.54 us (9%)
  other arithmetic  2.71 us (3%)
  matrix products  1.87 us (2%)
    pallas_call x1, Pallas kernels, fused_on_device(): pl.pallas_call(lambda *refs: cell_kernel(slabs, points, *refs), out_shape...  87.3 us
    unnamed x23, local copies, waits for them, and re-layouts  6.75 us

profile of v1, /device:TPU:0, one launch (start us, length us, event | category | flops | bytes accessed | tf_op | source)
XLA Modules:
  0.0 102.2 jit_solution(16756977626033229755)
XLA Ops:
  0.6 0.7 fusion.4
  1.4 0.8 multiply_reduce_fusion.3
  2.3 0.8 multiply_reduce_fusion.1
  3.2 1.4 %copy-done = f32[1,6,16,4096]{3,2,1,0:T(8,128)S(1)} copy-done((f32[1,6,16,4096]{3,2,1,0:T(8,128)S(1)}, f32[1,6,16,4096]{3,2,1,0:T(8,128)}, u32[]{:S(2)}) %copy-start) | copy-done | bytes 1572888
  4.6 1.1 %copy-done.1 = s32[1,3,16,4096]{3,2,1,0:T(8,128)S(1)} copy-done((s32[1,3,16,4096]{3,2,1,0:T(8,128)S(1)}, s32[1,3,16,4096]{3,2,1,0:T(8,128)}, u32[]{:S(2)}) %copy-start.1) | copy-done | bytes 786456
  5.7 1.0 %copy-done.2 = bf16[2,2,256,256]{3,2,1,0:T(8,128)(2,1)S(1)} copy-done((bf16[2,2,256,256]{3,2,1,0:T(8,128)(2,1)S(1)}, bf16[2,2,256,256]{3,2,1,0:T(8,128)(2,1)}, u32[]{:S(2)}) %copy-start.2) | copy-done | bytes 524312
  6.7 0.9 copy-done.3
  7.7 0.9 copy-done.4
  8.6 0.7 copy-done.5
  9.3 87.3 %shard_map.156 = f32[8,32,128]{2,1,0:T(8,128)S(1)} custom-call(f32[6]{0:T(128)S(1)} %fusion.13.refs_0_, s32[16,4096]{1,0:T(8,128)S(1)} %copy-done.3, s32[3,16,4096]{2,1,0:T(8,128)S(1)} %bitcast.41, f32[6,16,4096]{2,1,0:T(8,128)S(1)} %bitcast.40, bf16[2,2,256,256]{3,2,1,0:T(8,128)(2,1)S(1)} %copy-done.2, bf16[2,2,128,128]{3,2,1,0:T(8,128)(2,1)S(1)} %copy-done.4, ...), custom_call_target="tpu_custom_call" | custom-call | tf_op jit(solution)/shard_map/pallas_call | solution.py:808
  96.9 0.5 constant_dynamic-slice_fusion.1
  97.4 0.2 slice_reduce_fusion
  97.8 0.1 stack.4
  98.2 0.6 copy.29
  98.9 0.1 multiply_reduce_fusion.2
  99.1 0.8 fusion.6
  99.9 0.2 convolution_bitcast_fusion.1
  100.1 0.2 convolution_bitcast_fusion.2
  100.3 0.1 reshape.254
  100.4 0.2 copy.26
  100.6 0.4 fusion.8
  101.0 0.2 convolution_bitcast_fusion
  101.3 0.2 copy.28
  101.5 0.7 reshape.251
  (32 shorter events, 1.1 us)
Async XLA Ops:
  3.1 1.4 %copy-start = (f32[1,6,16,4096]{3,2,1,0:T(8,128)S(1)}, f32[1,6,16,4096]{3,2,1,0:T(8,128)}, u32[]{:S(2)}) copy-start(f32[1,6,16,4096]{3,2,1,0:T(8,128)} %param.15) | copy-start | bytes 4718596
  4.6 1.1 %copy-start.1 = (s32[1,3,16,4096]{3,2,1,0:T(8,128)S(1)}, s32[1,3,16,4096]{3,2,1,0:T(8,128)}, u32[]{:S(2)}) copy-start(s32[1,3,16,4096]{3,2,1,0:T(8,128)} %param.14) | copy-start | bytes 2359300
  5.7 1.0 %copy-start.2 = (bf16[2,2,256,256]{3,2,1,0:T(8,128)(2,1)S(1)}, bf16[2,2,256,256]{3,2,1,0:T(8,128)(2,1)}, u32[]{:S(2)}) copy-start(bf16[2,2,256,256]{3,2,1,0:T(8,128)(2,1)} %constant.39.clone.refs_4_) | copy-start | bytes 1572868
  6.7 0.9 copy-start.3
  7.7 0.9 copy-start.4
  8.6 0.7 copy-start.5
  9.3 88.7 %copy-start.9 = (f32[6]{0:T(128)S(1)}, f32[6]{0:T(128)}, u32[]{:S(2)}) copy-start(f32[6]{0:T(128)} %constant.42.clone) | copy-start | bytes 76
  9.3 88.8 %copy-start.10 = (f32[6]{0:T(128)S(1)}, f32[6]{0:T(128)}, u32[]{:S(2)}) copy-start(f32[6]{0:T(128)} %constant.43.clone) | copy-start | bytes 76
  9.3 89.6 %copy-start.7 = (f32[48,24]{0,1:T(8,128)S(1)}, f32[48,24]{0,1:T(8,128)}, u32[]{:S(2)}) copy-start(f32[48,24]{0,1:T(8,128)} %constant.44.clone) | copy-start | bytes 13828
  9.3 89.8 %copy-start.8 = (s32[1,8]{1,0:T(1,128)S(1)}, s32[1,8]{1,0:T(1,128)}, u32[]{:S(2)}) copy-start(s32[1,8]{1,0:T(1,128)} %param.17) | copy-start | bytes 100
  9.3 90.6 %copy-start.6 = (f32[8,6,24]{2,1,0:T(8,128)S(1)}, f32[8,6,24]{2,1,0:T(8,128)}, u32[]{:S(2)}) copy-start(f32[8,6,24]{2,1,0:T(8,128)} %constant.38.clone) | copy-start | bytes 13828

commit v2 on v1

--- a/solution.py
+++ b/solution.py
@@ -835,7 +835,7 @@
             pltpu.SemaphoreType.DMA((points - 1,)),
         ],
         compiler_params=pltpu.CompilerParams(
-            collective_id=0, has_side_effects=True, vmem_limit_bytes=40 * 1024 * 1024
+            collective_id=0, has_side_effects=True, vmem_limit_bytes=60 * 1024 * 1024
         ),
     )(
         macro_strain,

time: 103 us -> 98.7 us (0.958)
  local copies, waits for them, and re-layouts: 9.54 us -> 3.91 us
    unnamed x23 -> x11, local copies, waits for them, and re-layouts: 6.75 us -> 0.6 us
where the time goes in v2:
time: 98.7 us; the launch traced here: 98.4 us
  Pallas kernels  88.2 us (89%)
  local copies, waits for them, and re-layouts  3.91 us (4%)
  other arithmetic  3.62 us (4%)
  matrix products  1.87 us (2%)
    pallas_call x1, Pallas kernels, fused_on_device(): pl.pallas_call(lambda *refs: cell_kernel(slabs, points, *refs), out_shape...  88.2 us

profile of v2, /device:TPU:0, one launch (start us, length us, event | category | flops | bytes accessed | tf_op | source)
XLA Modules:
  0.0 98.4 jit_solution(8659722848597442593)
XLA Ops:
  0.6 0.7 fusion.4
  1.4 0.8 multiply_reduce_fusion.3
  2.1 0.1 copy.24
  2.2 0.1 mul.103
  2.3 0.8 multiply_reduce_fusion.1
  3.1 0.5 fusion.13.refs_0_
  3.7 88.2 %shard_map.156 = f32[8,32,128]{2,1,0:T(8,128)} custom-call(f32[6]{0:T(128)} %fusion.13.refs_0_, s32[16,4096]{1,0:T(8,128)} %refs_1_.1, s32[3,16,4096]{2,1,0:T(8,128)} %bitcast.41, f32[6,16,4096]{2,1,0:T(8,128)} %bitcast.40, bf16[2,2,256,256]{3,2,1,0:T(8,128)(2,1)} %constant.39.clone.refs_4_, bf16[2,2,128,128]{3,2,1,0:T(8,128)(2,1)} %constant.40.clone.refs_5_, ...), custom_call_target="tpu_custom_call" | custom-call | tf_op jit(solution)/shard_map/pallas_call | solution.py:808
  91.9 1.0 %multiply_reduce_fusion = f32[8,32]{1,0:T(8,128)S(1)} fusion(f32[8,32,128]{2,1,0:T(8,128)} %shard_map.156), kind=kLoop, calls=%fused_computation.3 | loop fusion | flops 256 | bytes 2048 | tf_op jit(solution)/shard_map/div | solution.py:849
  93.0 0.5 constant_dynamic-slice_fusion.1
  93.5 0.2 slice_reduce_fusion
  94.0 0.1 stack.4
  94.3 0.1 subtract_multiply_fusion
  94.4 0.6 copy.29
  95.0 0.1 multiply_reduce_fusion.2
  95.1 0.1 reshape.248
  95.2 0.8 fusion.6
  96.0 0.2 convolution_bitcast_fusion.1
  96.2 0.2 convolution_bitcast_fusion.2
  96.4 0.1 reshape.254
  96.6 0.2 copy.26
  96.8 0.4 fusion.8
  97.2 0.2 convolution_bitcast_fusion
  97.4 0.2 copy.28
  97.7 0.7 reshape.251
  (20 shorter events, 0.6 us)
Async XLA Ops:
  3.7 90.5 %copy-start.3 = (f32[6]{0:T(128)S(1)}, f32[6]{0:T(128)}, u32[]{:S(2)}) copy-start(f32[6]{0:T(128)} %constant.42.clone) | copy-start | bytes 76
  3.7 90.6 %copy-start.4 = (f32[6]{0:T(128)S(1)}, f32[6]{0:T(128)}, u32[]{:S(2)}) copy-start(f32[6]{0:T(128)} %constant.43.clone) | copy-start | bytes 76
  3.7 91.4 %copy-start.1 = (f32[48,24]{0,1:T(8,128)S(1)}, f32[48,24]{0,1:T(8,128)}, u32[]{:S(2)}) copy-start(f32[48,24]{0,1:T(8,128)} %constant.44.clone) | copy-start | bytes 13828
  3.7 91.6 %copy-start.2 = (s32[1,8]{1,0:T(1,128)S(1)}, s32[1,8]{1,0:T(1,128)}, u32[]{:S(2)}) copy-start(s32[1,8]{1,0:T(1,128)} %param.17) | copy-start | bytes 100
  3.7 92.4 %copy-start = (f32[8,6,24]{2,1,0:T(8,128)S(1)}, f32[8,6,24]{2,1,0:T(8,128)}, u32[]{:S(2)}) copy-start(f32[8,6,24]{2,1,0:T(8,128)} %constant.38.clone) | copy-start | bytes 13828

commit v3 on v2

--- a/solution.py
+++ b/solution.py
@@ -565,11 +565,11 @@
     def plane_forward(iteration, part):
         picked = part_rows(part)
 
-        @pl.loop(0, ROUGH // 4)
+        @pl.loop(0, ROUGH // 8)
         def _(batch):
             pieces = []
-            for inner in range(4):
-                at = lane_block(batch * 4 + inner)
+            for inner in range(8):
+                at = lane_block(batch * 8 + inner)
                 pieces += voxel_law(
                     [elastic[n, picked, at] for n in range(6)],
                     phase_ref[picked, at],
@@ -580,11 +580,11 @@
             result = (
                 mul(high, depth_ref[0, 0]) + mul(low, depth_ref[0, 0]) + mul(high, depth_ref[0, 1])
             )
-            for inner in range(4):
+            for inner in range(8):
                 for n in range(6):
                     first = (inner * 6 + n) * 8
-                    planes[n, 0, batch * 4 + inner, picked, :] = result[first : first + 8, :LANES]
-                    planes[n, 1, batch * 4 + inner, picked, :] = result[first : first + 8, LANES:]
+                    planes[n, 0, batch * 8 + inner, picked, :] = result[first : first + 8, :LANES]
+                    planes[n, 1, batch * 8 + inner, picked, :] = result[first : first + 8, LANES:]
 
         sixteen(planes, -1, part)
 
@@ -631,14 +631,14 @@
 
         sixteen(planes_back, 1, part)
 
-        @pl.loop(0, ROUGH // 4)
+        @pl.loop(0, ROUGH // 8)
         def _(batch):
             stacked = jnp.concatenate(
                 [
                     jnp.concatenate(
                         [
-                            planes_back[n, side, batch * 4 + inner, picked, :]
-                            for inner in range(4)
+                            planes_back[n, side, batch * 8 + inner, picked, :]
+                            for inner in range(8)
                             for n in range(6)
                         ],
                         axis=0,
@@ -651,8 +651,8 @@
             result = (
                 mul(high, depth_ref[1, 0]) + mul(low, depth_ref[1, 0]) + mul(high, depth_ref[1, 1])
             )
-            for inner in range(4):
-                at = lane_block(batch * 4 + inner)
+            for inner in range(8):
+                at = lane_block(batch * 8 + inner)
                 for n in range(6):
                     first = (inner * 6 + n) * 8
                     elastic[n, picked, at] = elastic[n, picked, at] - result[first : first + 8]

time: 98.7 us -> 98 us (level)
  no operation moved by 1% of the time
where the time goes in v3:
time: 98 us; the launch traced here: 97.7 us
  Pallas kernels  87.6 us (89%)
  local copies, waits for them, and re-layouts  3.91 us (4%)
  other arithmetic  3.62 us (4%)
  matrix products  1.87 us (2%)
    pallas_call x1, Pallas kernels, fused_on_device(): pl.pallas_call(lambda *refs: cell_kernel(slabs, points, *refs), out_shape...  87.6 us

profile of v3, /device:TPU:0, one launch (start us, length us, event | category | flops | bytes accessed | tf_op | source)
XLA Modules:
  0.0 97.7 jit_solution(8810114209882406798)
XLA Ops:
  0.6 0.7 fusion.4
  1.4 0.8 multiply_reduce_fusion.3
  2.1 0.1 copy.24
  2.2 0.1 mul.103
  2.3 0.8 multiply_reduce_fusion.1
  3.1 0.5 fusion.13.refs_0_
  3.7 87.6 %shard_map.156 = f32[8,32,128]{2,1,0:T(8,128)} custom-call(f32[6]{0:T(128)} %fusion.13.refs_0_, s32[16,4096]{1,0:T(8,128)} %refs_1_.1, s32[3,16,4096]{2,1,0:T(8,128)} %bitcast.41, f32[6,16,4096]{2,1,0:T(8,128)} %bitcast.40, bf16[2,2,256,256]{3,2,1,0:T(8,128)(2,1)} %constant.39.clone.refs_4_, bf16[2,2,128,128]{3,2,1,0:T(8,128)(2,1)} %constant.40.clone.refs_5_, ...), custom_call_target="tpu_custom_call" | custom-call | tf_op jit(solution)/shard_map/pallas_call | solution.py:808
  91.3 1.0 %multiply_reduce_fusion = f32[8,32]{1,0:T(8,128)S(1)} fusion(f32[8,32,128]{2,1,0:T(8,128)} %shard_map.156), kind=kLoop, calls=%fused_computation.3 | loop fusion | flops 256 | bytes 2048 | tf_op jit(solution)/shard_map/div | solution.py:849
  92.3 0.5 constant_dynamic-slice_fusion.1
  92.9 0.2 slice_reduce_fusion
  93.3 0.1 stack.4
  93.6 0.1 subtract_multiply_fusion
  93.7 0.6 copy.29
  94.4 0.1 multiply_reduce_fusion.2
  94.5 0.1 reshape.248
  94.6 0.8 fusion.6
  95.4 0.2 convolution_bitcast_fusion.1
  95.6 0.2 convolution_bitcast_fusion.2
  95.8 0.1 reshape.254
  95.9 0.2 copy.26
  96.1 0.4 fusion.8
  96.5 0.2 convolution_bitcast_fusion
  96.8 0.2 copy.28
  97.0 0.7 reshape.251
  (20 shorter events, 0.6 us)
Async XLA Ops:
  3.7 89.9 %copy-start.3 = (f32[6]{0:T(128)S(1)}, f32[6]{0:T(128)}, u32[]{:S(2)}) copy-start(f32[6]{0:T(128)} %constant.42.clone) | copy-start | bytes 76
  3.7 89.9 %copy-start.4 = (f32[6]{0:T(128)S(1)}, f32[6]{0:T(128)}, u32[]{:S(2)}) copy-start(f32[6]{0:T(128)} %constant.43.clone) | copy-start | bytes 76
  3.7 90.7 %copy-start.1 = (f32[48,24]{0,1:T(8,128)S(1)}, f32[48,24]{0,1:T(8,128)}, u32[]{:S(2)}) copy-start(f32[48,24]{0,1:T(8,128)} %constant.44.clone) | copy-start | bytes 13828
  3.7 90.9 %copy-start.2 = (s32[1,8]{1,0:T(1,128)S(1)}, s32[1,8]{1,0:T(1,128)}, u32[]{:S(2)}) copy-start(s32[1,8]{1,0:T(1,128)} %param.17) | copy-start | bytes 100
  3.7 91.7 %copy-start = (f32[8,6,24]{2,1,0:T(8,128)S(1)}, f32[8,6,24]{2,1,0:T(8,128)}, u32[]{:S(2)}) copy-start(f32[8,6,24]{2,1,0:T(8,128)} %constant.38.clone) | copy-start | bytes 13828
